TPU v7x, 32 devices: a whole 2x2x4 slice. The times are simulated.
32 devices in a mesh: ctx: 16 (over z, x, core), head: 2 (over y).
Axes of the slice: x: 2, y: 2, z: 4, core: 2. Of those that a mesh axis runs over, the one named last changes fastest.
Arguments:
- queries: bfloat16 [4096, 16, 128], P(('ctx', 'head')), may hold values from -8 to 8
- keys: bfloat16 [4096, 16, 128], P(('ctx', 'head')), may hold values from -6 to 6
- values: bfloat16 [4096, 16, 128], P(('ctx', 'head')), may hold values from -6 to 6
- out_grad: bfloat16 [4096, 16, 128], P(('ctx', 'head')), may hold values from -6 to 6
- block_lists: int32 [16, 3], P('ctx'), may hold values from 0 to 15, as said below
Outputs:
- attended: bfloat16 [4096, 16, 128], P(('ctx', 'head'))
- grad_query: bfloat16 [4096, 16, 128], P(('ctx', 'head'))
- grad_key: bfloat16 [4096, 16, 128], P(('ctx', 'head'))
- grad_value: bfloat16 [4096, 16, 128], P(('ctx', 'head'))
Inputs may be any that keep to these rules, and one draw needn't show every extreme that they name: `block_lists`: row b begins with b; its other entries are distinct blocks among b - 3 to b - 1, as many of them as exist up to 2, and b again where fewer exist.
All inputs are finite; a program needn't handle non-finite values.
Results may differ from a plain program's by a relative error of at most 0.015.
Values may be sent and summed in bfloat16 or wider, within the bound.
A program may use at most 64 MiB of HBM per device.

v0:
```python
import math

import jax
import jax.numpy as jnp
from jax import lax
from jax.sharding import PartitionSpec as P

R = 3


def from_behind(block, axis, distance):
    devices = range(lax.axis_size(axis))
    route = [(i - distance, i) for i in devices if i - distance in devices]
    return lax.ppermute(block, axis, route)


def attend(query_rows, key_window, value_window, grad_rows, allowed):
    score_scale = 1.0 / math.sqrt(query_rows.shape[-1])
    scores = (
        jnp.einsum("thd,shd->hts", query_rows, key_window, preferred_element_type=jnp.float32)
        * score_scale
    )
    scores = jnp.where(allowed[None], scores, -jnp.inf)
    highest = jnp.max(scores, axis=2, keepdims=True)
    weights = jnp.exp(scores - highest)
    probability = weights / jnp.sum(weights, axis=2, keepdims=True)
    probs_low = probability.astype(jnp.bfloat16)
    attended = jnp.einsum(
        "hts,shd->thd", probs_low, value_window, preferred_element_type=jnp.float32
    ).astype(jnp.bfloat16)
    grad_probs = jnp.einsum(
        "thd,shd->hts", grad_rows, value_window, preferred_element_type=jnp.float32
    )
    centre = jnp.sum(grad_rows.astype(jnp.float32) * attended.astype(jnp.float32), axis=2).T[
        :, :, None
    ]
    grad_scores = (probability * (grad_probs - centre)).astype(jnp.bfloat16)
    grad_query = (
        jnp.einsum("hts,shd->thd", grad_scores, key_window, preferred_element_type=jnp.float32)
        * score_scale
    ).astype(jnp.bfloat16)
    key_terms = (
        jnp.einsum("hts,thd->shd", grad_scores, query_rows, preferred_element_type=jnp.float32)
        * score_scale
    )
    value_terms = jnp.einsum(
        "hts,thd->shd", probs_low, grad_rows, preferred_element_type=jnp.float32
    )
    return (attended, grad_query, key_terms, value_terms)


def block_mask(block_permitted, tile_lower_mask, length):
    row_ids = jnp.arange(length)
    lower_tri = row_ids[:, None] >= row_ids[None, :]
    allowed = block_permitted[None, :, None] & (
        (~tile_lower_mask)[None, :, None] | lower_tri[:, None, :]
    )
    return allowed.reshape(length, block_permitted.shape[0] * length)


def local(queries, keys, values, out_grad, block_lists):
    query_rows, key_rows, value_rows, grad_rows = (
        lax.all_to_all(queries, "head", split_axis=1, concat_axis=0, tiled=True),
        lax.all_to_all(keys, "head", split_axis=1, concat_axis=0, tiled=True),
        lax.all_to_all(values, "head", split_axis=1, concat_axis=0, tiled=True),
        lax.all_to_all(out_grad, "head", split_axis=1, concat_axis=0, tiled=True),
    )
    length = query_rows.shape[0]
    head_count = query_rows.shape[1]
    width = query_rows.shape[2]
    position = lax.axis_index("ctx")
    listing = block_lists[0]
    key_tiles = [key_rows]
    value_tiles = [value_rows]
    held_key, held_value = (key_rows, value_rows)
    for distance in range(1, R + 1):
        held_key, held_value = from_behind((held_key, held_value), "ctx", 1)
        key_tiles.append(held_key)
        value_tiles.append(held_value)
    offsets = jnp.arange(R + 1, dtype=jnp.int32)
    candidate_block = position - offsets
    block_permitted = jnp.any(candidate_block[:, None] == listing[None, :], axis=1) & (
        candidate_block >= 0
    )
    tile_lower_mask = offsets == 0
    key_window = jnp.concatenate(key_tiles, axis=0)
    value_window = jnp.concatenate(value_tiles, axis=0)
    count = key_window.shape[0] // length
    allowed = block_mask(block_permitted, tile_lower_mask, length)
    attended, grad_query, key_terms, value_terms = attend(
        query_rows, key_window, value_window, grad_rows, allowed
    )
    key_terms = key_terms.reshape(count, length, head_count, width)
    value_terms = value_terms.reshape(count, length, head_count, width)
    key_total = key_terms[0]
    value_total = value_terms[0]
    for distance in range(1, R + 1):
        back_key, back_value = from_behind(
            (key_terms[distance].astype(jnp.bfloat16), value_terms[distance].astype(jnp.bfloat16)),
            "ctx",
            -distance,
        )
        key_total = key_total + back_key.astype(jnp.float32)
        value_total = value_total + back_value.astype(jnp.float32)
    return (
        lax.all_to_all(attended, "head", split_axis=0, concat_axis=1, tiled=True),
        lax.all_to_all(grad_query, "head", split_axis=0, concat_axis=1, tiled=True),
        lax.all_to_all(
            key_total.astype(jnp.bfloat16), "head", split_axis=0, concat_axis=1, tiled=True
        ),
        lax.all_to_all(
            value_total.astype(jnp.bfloat16), "head", split_axis=0, concat_axis=1, tiled=True
        ),
    )


def solution(mesh):
    placed = (
        P(("ctx", "head"), None, None),
        P(("ctx", "head"), None, None),
        P(("ctx", "head"), None, None),
        P(("ctx", "head"), None, None),
        P("ctx", None),
    )
    return jax.shard_map(
        local,
        mesh=mesh,
        in_specs=placed,
        out_specs=(
            P(("ctx", "head"), None, None),
            P(("ctx", "head"), None, None),
            P(("ctx", "head"), None, None),
            P(("ctx", "head"), None, None),
        ),
        check_vma=False,
    )
```

profile of v0, /device:TPU:10, one launch (start us, length us, event | category | flops | bytes accessed | tf_op | source)
XLA Modules:
  0.0 160.8 jit_solution(1103698851266385415)
XLA Ops:
  0.6 1.2 copy.47
  1.9 10.8 %all_to_all.144 = bf16[128,16,128]{2,0,1:T(8,128)(2,1)S(1)} all-to-all(bf16[128,16,128]{2,0,1:T(8,128)(2,1)S(1)} %copy.47), channel_id=1, replica_groups=mesh['ctx'=16,'head'=2] {'head'}, dimensions={1} | all-to-all | bytes 1048576 | tf_op jit(solution)/shard_map/all_to_all | solution.py:64
  12.7 1.9 %collective-permute-start.3 = (bf16[256,8,128]{2,0,1:T(8,128)(2,1)S(1)}, bf16[256,8,128]{2,0,1:T(8,128)(2,1)}, u32[]{:S(2)}, u32[]{:S(2)}) collective-permute-start(bf16[256,8,128]{2,0,1:T(8,128)(2,1)S(1)} %bitcast.94), channel_id=1, source_target_pairs={{0,2},{2,4},{4,6},{6,8},{8,10},{10,12},{12,14},{14,16},{16,18},{18... | collective-permute-start | bytes 1572872 | tf_op jit(solution)/shard_map/ppermute | solution.py:14
  14.7 1.2 copy.45
  15.9 11.2 %all_to_all.145 = bf16[128,16,128]{2,0,1:T(8,128)(2,1)S(1)} all-to-all(bf16[128,16,128]{2,0,1:T(8,128)(2,1)S(1)} %copy.45), channel_id=1, replica_groups=mesh['ctx'=16,'head'=2] {'head'}, dimensions={1} | all-to-all | bytes 1048576 | tf_op jit(solution)/shard_map/all_to_all | solution.py:65
  27.8 2.4 %collective-permute-start = (bf16[256,8,128]{0,2,1:T(8,128)(2,1)S(1)}, bf16[256,8,128]{0,2,1:T(8,128)(2,1)}, u32[]{:S(2)}, u32[]{:S(2)}) collective-permute-start(bf16[256,8,128]{0,2,1:T(8,128)(2,1)S(1)} %all_to_all.107), channel_id=1, source_target_pairs={{0,2},{2,4},{4,6},{6,8},{8,10},{10,12},{12,14},{14,16},{16,18},{18... | collective-permute-start | bytes 1572872 | tf_op jit(solution)/shard_map/ppermute | solution.py:14
  30.2 3.2 %collective-permute-start.4 = (bf16[256,8,128]{2,0,1:T(8,128)(2,1)}, bf16[256,8,128]{2,0,1:T(8,128)(2,1)}, u32[]{:S(2)}, u32[]{:S(2)}) collective-permute-start(bf16[256,8,128]{2,0,1:T(8,128)(2,1)} %collective-permute-done.3), channel_id=1, source_target_pairs={{0,2},{2,4},{4,6},{6,8},{8,10},{10,12},{12,14},{14,16},{16,18},{18... | collective-permute-start | bytes 1572872 | tf_op jit(solution)/shard_map/ppermute | solution.py:14
  33.4 0.9 copy.49
  34.3 3.5 %all-to-all-start.2 = ((bf16[128,16,128]{2,0,1:T(8,128)(2,1)}), bf16[128,16,128]{2,0,1:T(8,128)(2,1)S(1)}, u32[]{:S(2)}, u32[]{:S(2)}) async-start(bf16[128,16,128]{2,0,1:T(8,128)(2,1)} %copy.49), calls=%async_computation.2 | async-start | bytes 1048576 | tf_op jit(solution)/shard_map/all_to_all | solution.py:63
  37.8 0.9 copy.54
  38.9 2.3 %collective-permute-start.1 = (bf16[256,8,128]{0,2,1:T(8,128)(2,1)}, bf16[256,8,128]{0,2,1:T(8,128)(2,1)}, u32[]{:S(2)}, u32[]{:S(2)}) collective-permute-start(bf16[256,8,128]{0,2,1:T(8,128)(2,1)} %collective-permute-done), channel_id=1, source_target_pairs={{0,2},{2,4},{4,6},{6,8},{8,10},{10,12},{12,14},{14,16},{16,18},{18... | collective-permute-start | bytes 1572872 | tf_op jit(solution)/shard_map/ppermute | solution.py:14
  41.2 5.3 %all-to-all-done.2 = bf16[128,16,128]{2,0,1:T(8,128)(2,1)S(1)} async-done(((bf16[128,16,128]{2,0,1:T(8,128)(2,1)}), bf16[128,16,128]{2,0,1:T(8,128)(2,1)S(1)}, u32[]{:S(2)}, u32[]{:S(2)}) %all-to-all-start.2) | async-done | bytes 524320 | tf_op jit(solution)/shard_map/all_to_all | solution.py:63
  46.6 3.5 %all-to-all-start.4 = ((bf16[128,16,128]{2,0,1:T(8,128)(2,1)}), bf16[128,16,128]{2,0,1:T(8,128)(2,1)S(1)}, u32[]{:S(2)}, u32[]{:S(2)}) async-start(bf16[128,16,128]{2,0,1:T(8,128)(2,1)} %copy.54), calls=%async_computation.4 | async-start | bytes 1048576 | tf_op jit(solution)/shard_map/all_to_all | solution.py:66
  50.1 1.9 %collective-permute-start.5 = (bf16[256,8,128]{2,0,1:T(8,128)(2,1)}, bf16[256,8,128]{2,0,1:T(8,128)(2,1)}, u32[]{:S(2)}, u32[]{:S(2)}) collective-permute-start(bf16[256,8,128]{2,0,1:T(8,128)(2,1)} %collective-permute-done.4), channel_id=1, source_target_pairs={{0,2},{2,4},{4,6},{6,8},{8,10},{10,12},{12,14},{14,16},{16,18},{18... | collective-permute-start | bytes 1572872 | tf_op jit(solution)/shard_map/ppermute | solution.py:14
  53.4 4.7 %all-to-all-done.4 = bf16[128,16,128]{2,0,1:T(8,128)(2,1)S(1)} async-done(((bf16[128,16,128]{2,0,1:T(8,128)(2,1)}), bf16[128,16,128]{2,0,1:T(8,128)(2,1)S(1)}, u32[]{:S(2)}, u32[]{:S(2)}) %all-to-all-start.4) | async-done | bytes 524320 | tf_op jit(solution)/shard_map/all_to_all | solution.py:66
  59.0 1.1 constant_dynamic-update-slice_fusion.2
  60.1 1.9 %collective-permute-start.2 = (bf16[256,8,128]{0,2,1:T(8,128)(2,1)}, bf16[256,8,128]{0,2,1:T(8,128)(2,1)S(1)}, u32[]{:S(2)}, u32[]{:S(2)}) collective-permute-start(bf16[256,8,128]{0,2,1:T(8,128)(2,1)} %collective-permute-done.1), channel_id=1, source_target_pairs={{0,2},{2,4},{4,6},{6,8},{8,10},{10,12},{12,14},{14,16},{16,18},{18... | collective-permute-start | bytes 1572872 | tf_op jit(solution)/shard_map/ppermute | solution.py:14
  62.0 1.1 constant_dynamic-update-slice_fusion.1
  63.1 7.6 %fusion.23 = (f32[8,256]{1,0:T(8,128)S(1)}, f32[8,256,1024]{1,2,0:T(8,128)}) fusion(pred[256,1024]{0,1:T(8,128)(4,1)S(1)} %fusion.16, bf16[256,8,128]{2,0,1:T(8,128)(2,1)} %bitcast.92, bf16[256,8,128]{2,0,1:T(8,128)(2,1)} %collective-permute-done.5, bf16[256,8,128]{2,0,1:T(8,128)(2,1)} %collective-permute-done.4, ...), kind=kOutput, calls=%fused_computation.48 | convolution fusion | flops 553649152 | bytes 11280384 | tf_op jit(solution)/shard_map/sub | solution.py:25
  70.7 4.3 %fusion.6 = bf16[8,256,1024]{1,2,0:T(8,128)(2,1)S(1)} fusion(f32[8,256,1024]{1,2,0:T(8,128)} %get-tuple-element.11, f32[8,256]{1,0:T(8,128)S(1)} %get-tuple-element.10), kind=kLoop, calls=%fused_computation.11 | loop fusion | flops 4194304 | bytes 12591104 | tf_op jit(solution)/shard_map/convert_element_type | solution.py:27
  76.6 1.7 %fusion.1 = bf16[8,256,1024]{1,2,0:T(8,128)(2,1)S(1)} fusion(f32[8,256]{1,0:T(8,128)S(1)} %bitcast.101, f32[8,256,1024]{1,2,0:T(8,128)S(1)} %bitcast.81, f32[8,256]{1,0:T(8,128)S(1)} %get-tuple-element.10, bf16[1024,8,128]{0,2,1:T(8,128)(2,1)S(1)} %constant_dynamic-update-slice_fusion, bf16[256,8,128]{0,2,1:T(8,128)(2,1)S(1)} %all_to_all.123), kind=kOutput, calls=%fused_computation.2 | convolution fusion | flops 545259520 | bytes 15220736 | tf_op jit(solution)/shard_map/thd,shd->hts/dot_general | solution.py:31
  78.3 3.2 %fusion.24 = (bf16[1024,8,128]{2,0,1:T(8,128)(2,1)S(1)}, f32[1024,8,128]{2,0,1:T(8,128)}) fusion(bf16[8,256,1024]{1,2,0:T(8,128)(2,1)S(1)} %fusion.1, bf16[256,8,128]{2,0,1:T(8,128)(2,1)S(1)} %bitcast.93), kind=kOutput, calls=%fused_computation.49 | convolution fusion | flops 538968064 | bytes 11010048 | tf_op jit(solution)/shard_map/hts,thd->shd/dot_general | solution.py:43
  81.5 1.2 fusion.22
  82.7 3.6 %collective-permute-start.6 = (bf16[256,8,128]{2,0,1:T(8,128)(2,1)}, bf16[256,8,128]{2,0,1:T(8,128)(2,1)}, u32[]{:S(2)}, u32[]{:S(2)}) collective-permute-start(bf16[256,8,128]{2,0,1:T(8,128)(2,1)} %get-tuple-element.7), channel_id=1, source_target_pairs={{2,0},{4,2},{6,4},{8,6},{10,8},{12,10},{14,12},{16,14},{18,16},{20... | collective-permute-start | bytes 1572872 | tf_op jit(solution)/shard_map/ppermute | solution.py:14
  86.4 1.9 %collective-permute-start.8 = (bf16[256,8,128]{2,0,1:T(8,128)(2,1)}, bf16[256,8,128]{2,0,1:T(8,128)(2,1)}, u32[]{:S(2)}, u32[]{:S(2)}) collective-permute-start(bf16[256,8,128]{2,0,1:T(8,128)(2,1)} %get-tuple-element.8), channel_id=1, source_target_pairs={{6,0},{8,2},{10,4},{12,6},{14,8},{16,10},{18,12},{20,14},{22,16},{... | collective-permute-start | bytes 1572872 | tf_op jit(solution)/shard_map/ppermute | solution.py:14
  88.3 3.6 %collective-permute-start.7 = (bf16[256,8,128]{2,0,1:T(8,128)(2,1)}, bf16[256,8,128]{2,0,1:T(8,128)(2,1)}, u32[]{:S(2)}, u32[]{:S(2)}) collective-permute-start(bf16[256,8,128]{2,0,1:T(8,128)(2,1)} %get-tuple-element.9), channel_id=1, source_target_pairs={{4,0},{6,2},{8,4},{10,6},{12,8},{14,10},{16,12},{18,14},{20,16},{2... | collective-permute-start | bytes 1572872 | tf_op jit(solution)/shard_map/ppermute | solution.py:14
  91.9 3.1 %fusion.9 = bf16[256,8,128]{0,2,1:T(8,128)(2,1)} fusion(bf16[8,256,1024]{1,2,0:T(8,128)(2,1)S(1)} %fusion.1, bf16[256,8,128]{2,0,1:T(8,128)(2,1)} %collective-permute-done.5, bf16[256,8,128]{2,0,1:T(8,128)(2,1)} %collective-permute-done.4, bf16[256,8,128]{2,0,1:T(8,128)(2,1)} %collective-permute-done.3, bf16[256,8,128]{2,0,1:T(8,128)(2,1)S(1)} %bitcast.96), kind=kOutput, calls=%fused_computation.18 | convolution fusion | flops 545783808 | bytes 6815744 | tf_op jit(solution)/shard_map/hts,shd->thd/dot_general | solution.py:39
  95.0 3.3 %fusion.25 = (bf16[1024,8,128]{2,0,1:T(8,128)(2,1)S(1)}, f32[1024,8,128]{2,0,1:T(8,128)}) fusion(bf16[8,256,1024]{1,2,0:T(8,128)(2,1)S(1)} %fusion.6, bf16[256,8,128]{0,2,1:T(8,128)(2,1)S(1)} %all_to_all.123), kind=kOutput, calls=%fused_computation.50 | convolution fusion | flops 537919488 | bytes 11010048 | tf_op jit(solution)/shard_map/hts,thd->shd/dot_general | solution.py:46
  98.3 2.1 %copy.60 = bf16[256,8,128]{2,1,0:T(8,128)(2,1)} copy(bf16[256,8,128]{0,2,1:T(8,128)(2,1)} %fusion.9) | data formatting | bytes 1048576 | tf_op jit(solution)/shard_map/convert_element_type | solution.py:41
  100.4 3.5 %all-to-all-start.5 = ((bf16[256,8,128]{2,1,0:T(8,128)(2,1)}), bf16[256,8,128]{2,1,0:T(8,128)(2,1)S(1)}, u32[]{:S(2)}, u32[]{:S(2)}) async-start(bf16[256,8,128]{2,1,0:T(8,128)(2,1)} %copy.60), calls=%async_computation.5 | async-start | bytes 1048576 | tf_op jit(solution)/shard_map/all_to_all | solution.py:107
  103.9 1.2 fusion.21
  105.1 2.0 %collective-permute-start.9 = (bf16[256,8,128]{2,0,1:T(8,128)(2,1)}, bf16[256,8,128]{2,0,1:T(8,128)(2,1)S(1)}, u32[]{:S(2)}, u32[]{:S(2)}) collective-permute-start(bf16[256,8,128]{2,0,1:T(8,128)(2,1)} %get-tuple-element.4), channel_id=1, source_target_pairs={{2,0},{4,2},{6,4},{8,6},{10,8},{12,10},{14,12},{16,14},{18,16},{20... | collective-permute-start | bytes 1572872 | tf_op jit(solution)/shard_map/ppermute | solution.py:14
  107.1 1.9 %collective-permute-start.11 = (bf16[256,8,128]{2,0,1:T(8,128)(2,1)}, bf16[256,8,128]{2,0,1:T(8,128)(2,1)S(1)}, u32[]{:S(2)}, u32[]{:S(2)}) collective-permute-start(bf16[256,8,128]{2,0,1:T(8,128)(2,1)} %get-tuple-element.5), channel_id=1, source_target_pairs={{6,0},{8,2},{10,4},{12,6},{14,8},{16,10},{18,12},{20,14},{22,16},{... | collective-permute-start | bytes 1572872 | tf_op jit(solution)/shard_map/ppermute | solution.py:14
  109.1 1.9 %collective-permute-start.10 = (bf16[256,8,128]{2,0,1:T(8,128)(2,1)}, bf16[256,8,128]{2,0,1:T(8,128)(2,1)}, u32[]{:S(2)}, u32[]{:S(2)}) collective-permute-start(bf16[256,8,128]{2,0,1:T(8,128)(2,1)} %get-tuple-element.6), channel_id=1, source_target_pairs={{4,0},{6,2},{8,4},{10,6},{12,8},{14,10},{16,12},{18,14},{20,16},{2... | collective-permute-start | bytes 1572872 | tf_op jit(solution)/shard_map/ppermute | solution.py:14
  111.0 1.1 copy.52
  112.6 3.5 %all-to-all-start.3 = ((bf16[256,8,128]{2,1,0:T(8,128)(2,1)}), bf16[256,8,128]{2,1,0:T(8,128)(2,1)S(1)}, u32[]{:S(2)}, u32[]{:S(2)}) async-start(bf16[256,8,128]{2,1,0:T(8,128)(2,1)} %copy.52), calls=%async_computation.3 | async-start | bytes 1048576 | tf_op jit(solution)/shard_map/all_to_all | solution.py:106
  116.1 6.5 %collective-permute-done.7 = bf16[256,8,128]{2,0,1:T(8,128)(2,1)} collective-permute-done((bf16[256,8,128]{2,0,1:T(8,128)(2,1)}, bf16[256,8,128]{2,0,1:T(8,128)(2,1)}, u32[]{:S(2)}, u32[]{:S(2)}) %collective-permute-start.7) | collective-permute-done | bytes 524320 | tf_op jit(solution)/shard_map/ppermute | solution.py:14
  122.6 1.9 %fusion.15 = bf16[256,8,128]{2,0,1:T(8,128)(2,1)S(1)} fusion(f32[1024,8,128]{2,0,1:T(8,128)} %get-tuple-element.15, bf16[256,8,128]{2,0,1:T(8,128)(2,1)} %collective-permute-done.8, bf16[256,8,128]{2,0,1:T(8,128)(2,1)} %collective-permute-done.7, bf16[256,8,128]{2,0,1:T(8,128)(2,1)} %collective-permute-done.6), kind=kLoop, calls=%fused_computation.26 | loop fusion | flops 1835008 | bytes 3145728 | tf_op jit(solution)/shard_map/convert_element_type | solution.py:109
  124.5 1.1 copy.62
  125.7 3.5 %all-to-all-start.6 = ((bf16[256,8,128]{2,1,0:T(8,128)(2,1)}), bf16[256,8,128]{2,1,0:T(8,128)(2,1)S(1)}, u32[]{:S(2)}, u32[]{:S(2)}) async-start(bf16[256,8,128]{2,1,0:T(8,128)(2,1)} %copy.62), calls=%async_computation.6 | async-start | bytes 1048576 | tf_op jit(solution)/shard_map/all_to_all | solution.py:108
  129.2 17.7 %collective-permute-done.10 = bf16[256,8,128]{2,0,1:T(8,128)(2,1)} collective-permute-done((bf16[256,8,128]{2,0,1:T(8,128)(2,1)}, bf16[256,8,128]{2,0,1:T(8,128)(2,1)}, u32[]{:S(2)}, u32[]{:S(2)}) %collective-permute-start.10) | collective-permute-done | bytes 524320 | tf_op jit(solution)/shard_map/ppermute | solution.py:14
  146.9 1.8 %fusion.12 = bf16[256,8,128]{2,0,1:T(8,128)(2,1)S(1)} fusion(f32[1024,8,128]{2,0,1:T(8,128)} %get-tuple-element.17, bf16[256,8,128]{2,0,1:T(8,128)(2,1)} %copy-done.5, bf16[256,8,128]{2,0,1:T(8,128)(2,1)} %collective-permute-done.10, bf16[256,8,128]{2,0,1:T(8,128)(2,1)S(1)} %collective-permute-done.9), kind=kLoop, calls=%fused_computation.22 | loop fusion | flops 1835008 | bytes 3145728 | tf_op jit(solution)/shard_map/convert_element_type | solution.py:112
  148.7 1.1 copy.65
  149.8 3.5 %all-to-all-start.7 = ((bf16[256,8,128]{2,1,0:T(8,128)(2,1)}), bf16[256,8,128]{2,1,0:T(8,128)(2,1)S(1)}, u32[]{:S(2)}, u32[]{:S(2)}) async-start(bf16[256,8,128]{2,1,0:T(8,128)(2,1)} %copy.65), calls=%async_computation.7 | async-start | bytes 1048576 | tf_op jit(solution)/shard_map/all_to_all | solution.py:111
  153.3 0.9 copy.79
  155.1 0.9 copy.78
  156.0 3.9 %all-to-all-done.7 = bf16[256,8,128]{2,1,0:T(8,128)(2,1)S(1)} async-done(((bf16[256,8,128]{2,1,0:T(8,128)(2,1)}), bf16[256,8,128]{2,1,0:T(8,128)(2,1)S(1)}, u32[]{:S(2)}, u32[]{:S(2)}) %all-to-all-start.7) | async-done | bytes 524320 | tf_op jit(solution)/shard_map/all_to_all | solution.py:111
  159.9 0.9 copy.77
  (52 shorter events, 6.1 us)
Async XLA Ops:
  0.6 32.7 %copy-start.1 = (bf16[128,16,128]{2,1,0:T(8,128)(2,1)S(1)}, bf16[128,16,128]{2,1,0:T(8,128)(2,1)}, u32[]{:S(2)}) copy-start(bf16[128,16,128]{2,1,0:T(8,128)(2,1)} %param.5) | copy-start | bytes 1572868
  1.9 35.9 %copy-start.2 = (bf16[128,16,128]{2,1,0:T(8,128)(2,1)S(1)}, bf16[128,16,128]{2,1,0:T(8,128)(2,1)}, u32[]{:S(2)}) copy-start(bf16[128,16,128]{2,1,0:T(8,128)(2,1)} %param.8) | copy-start | bytes 1572868
  12.7 26.1 %copy-start.6 = (s32[1,3]{1,0:T(1,128)S(1)}, s32[1,3]{1,0:T(1,128)}, u32[]{:S(2)}) copy-start(s32[1,3]{1,0:T(1,128)} %param.9) | copy-start | bytes 40
  12.7 33.9 %copy-start.3 = (bf16[128,2,8,128]{3,0,1,2:T(8,128)(2,1)}, bf16[128,2,8,128]{3,0,1,2:T(8,128)(2,1)S(1)}, u32[]{:S(2)}) copy-start(bf16[128,2,8,128]{3,0,1,2:T(8,128)(2,1)S(1)} %copy.48) | copy-start | bytes 1572868
  12.7 17.4 %collective-permute-start.3 = (bf16[256,8,128]{2,0,1:T(8,128)(2,1)S(1)}, bf16[256,8,128]{2,0,1:T(8,128)(2,1)}, u32[]{:S(2)}, u32[]{:S(2)}) collective-permute-start(bf16[256,8,128]{2,0,1:T(8,128)(2,1)S(1)} %bitcast.94), channel_id=1, source_target_pairs={{0,2},{2,4},{4,6},{6,8},{8,10},{10,12},{12,14},{14,16},{16,18},{18... | collective-permute-start | bytes 1572872 | tf_op jit(solution)/shard_map/ppermute | solution.py:14
  27.8 11.2 %collective-permute-start = (bf16[256,8,128]{0,2,1:T(8,128)(2,1)S(1)}, bf16[256,8,128]{0,2,1:T(8,128)(2,1)}, u32[]{:S(2)}, u32[]{:S(2)}) collective-permute-start(bf16[256,8,128]{0,2,1:T(8,128)(2,1)S(1)} %all_to_all.107), channel_id=1, source_target_pairs={{0,2},{2,4},{4,6},{6,8},{8,10},{10,12},{12,14},{14,16},{16,18},{18... | collective-permute-start | bytes 1572872 | tf_op jit(solution)/shard_map/ppermute | solution.py:14
  30.2 19.9 %collective-permute-start.4 = (bf16[256,8,128]{2,0,1:T(8,128)(2,1)}, bf16[256,8,128]{2,0,1:T(8,128)(2,1)}, u32[]{:S(2)}, u32[]{:S(2)}) collective-permute-start(bf16[256,8,128]{2,0,1:T(8,128)(2,1)} %collective-permute-done.3), channel_id=1, source_target_pairs={{0,2},{2,4},{4,6},{6,8},{8,10},{10,12},{12,14},{14,16},{16,18},{18... | collective-permute-start | bytes 1572872 | tf_op jit(solution)/shard_map/ppermute | solution.py:14
  34.3 12.3 %all-to-all-start.2 = ((bf16[128,16,128]{2,0,1:T(8,128)(2,1)}), bf16[128,16,128]{2,0,1:T(8,128)(2,1)S(1)}, u32[]{:S(2)}, u32[]{:S(2)}) async-start(bf16[128,16,128]{2,0,1:T(8,128)(2,1)} %copy.49), calls=%async_computation.2 | async-start | bytes 1048576 | tf_op jit(solution)/shard_map/all_to_all | solution.py:63
  38.9 21.2 %collective-permute-start.1 = (bf16[256,8,128]{0,2,1:T(8,128)(2,1)}, bf16[256,8,128]{0,2,1:T(8,128)(2,1)}, u32[]{:S(2)}, u32[]{:S(2)}) collective-permute-start(bf16[256,8,128]{0,2,1:T(8,128)(2,1)} %collective-permute-done), channel_id=1, source_target_pairs={{0,2},{2,4},{4,6},{6,8},{8,10},{10,12},{12,14},{14,16},{16,18},{18... | collective-permute-start | bytes 1572872 | tf_op jit(solution)/shard_map/ppermute | solution.py:14
  46.6 11.6 %all-to-all-start.4 = ((bf16[128,16,128]{2,0,1:T(8,128)(2,1)}), bf16[128,16,128]{2,0,1:T(8,128)(2,1)S(1)}, u32[]{:S(2)}, u32[]{:S(2)}) async-start(bf16[128,16,128]{2,0,1:T(8,128)(2,1)} %copy.54), calls=%async_computation.4 | async-start | bytes 1048576 | tf_op jit(solution)/shard_map/all_to_all | solution.py:66
  50.1 13.0 %collective-permute-start.5 = (bf16[256,8,128]{2,0,1:T(8,128)(2,1)}, bf16[256,8,128]{2,0,1:T(8,128)(2,1)}, u32[]{:S(2)}, u32[]{:S(2)}) collective-permute-start(bf16[256,8,128]{2,0,1:T(8,128)(2,1)} %collective-permute-done.4), channel_id=1, source_target_pairs={{0,2},{2,4},{4,6},{6,8},{8,10},{10,12},{12,14},{14,16},{16,18},{18... | collective-permute-start | bytes 1572872 | tf_op jit(solution)/shard_map/ppermute | solution.py:14
  60.1 14.9 %collective-permute-start.2 = (bf16[256,8,128]{0,2,1:T(8,128)(2,1)}, bf16[256,8,128]{0,2,1:T(8,128)(2,1)S(1)}, u32[]{:S(2)}, u32[]{:S(2)}) collective-permute-start(bf16[256,8,128]{0,2,1:T(8,128)(2,1)} %collective-permute-done.1), channel_id=1, source_target_pairs={{0,2},{2,4},{4,6},{6,8},{8,10},{10,12},{12,14},{14,16},{16,18},{18... | collective-permute-start | bytes 1572872 | tf_op jit(solution)/shard_map/ppermute | solution.py:14
  70.7 5.2 %slice-start = ((s8[8388608]{0:T(1024)(128)(4,1)}), s8[4194304]{0:T(1024)(128)(4,1)S(1)}, s32[]{:S(2)}) async-start(s8[8388608]{0:T(1024)(128)(4,1)} %bitcast.80), calls=%async_computation.8 | async-start | bytes 8388608
  70.7 5.9 %slice-start.1 = ((s8[8388608]{0:T(1024)(128)(4,1)}), s8[4194304]{0:T(1024)(128)(4,1)S(1)}, s32[]{:S(2)}) async-start(s8[8388608]{0:T(1024)(128)(4,1)} %bitcast.80), calls=%async_computation.9 | async-start | bytes 8388608
  76.6 1.7 %copy-start = (bf16[128,2,8,128]{3,0,1,2:T(8,128)(2,1)S(1)}, bf16[128,2,8,128]{3,0,1,2:T(8,128)(2,1)}, u32[]{:S(2)}) copy-start(bf16[128,2,8,128]{3,0,1,2:T(8,128)(2,1)} %copy.50) | copy-start | bytes 1572868
  78.3 13.6 %copy-start.4 = (bf16[128,2,8,128]{3,0,1,2:T(8,128)(2,1)S(1)}, bf16[128,2,8,128]{3,0,1,2:T(8,128)(2,1)}, u32[]{:S(2)}) copy-start(bf16[128,2,8,128]{3,0,1,2:T(8,128)(2,1)} %copy-done.3) | copy-start | bytes 1572868
  82.7 26.3 %collective-permute-start.6 = (bf16[256,8,128]{2,0,1:T(8,128)(2,1)}, bf16[256,8,128]{2,0,1:T(8,128)(2,1)}, u32[]{:S(2)}, u32[]{:S(2)}) collective-permute-start(bf16[256,8,128]{2,0,1:T(8,128)(2,1)} %get-tuple-element.7), channel_id=1, source_target_pairs={{2,0},{4,2},{6,4},{8,6},{10,8},{12,10},{14,12},{16,14},{18,16},{20... | collective-permute-start | bytes 1572872 | tf_op jit(solution)/shard_map/ppermute | solution.py:14
  86.4 29.7 %collective-permute-start.8 = (bf16[256,8,128]{2,0,1:T(8,128)(2,1)}, bf16[256,8,128]{2,0,1:T(8,128)(2,1)}, u32[]{:S(2)}, u32[]{:S(2)}) collective-permute-start(bf16[256,8,128]{2,0,1:T(8,128)(2,1)} %get-tuple-element.8), channel_id=1, source_target_pairs={{6,0},{8,2},{10,4},{12,6},{14,8},{16,10},{18,12},{20,14},{22,16},{... | collective-permute-start | bytes 1572872 | tf_op jit(solution)/shard_map/ppermute | solution.py:14
  88.3 34.2 %collective-permute-start.7 = (bf16[256,8,128]{2,0,1:T(8,128)(2,1)}, bf16[256,8,128]{2,0,1:T(8,128)(2,1)}, u32[]{:S(2)}, u32[]{:S(2)}) collective-permute-start(bf16[256,8,128]{2,0,1:T(8,128)(2,1)} %get-tuple-element.9), channel_id=1, source_target_pairs={{4,0},{6,2},{8,4},{10,6},{12,8},{14,10},{16,12},{18,14},{20,16},{2... | collective-permute-start | bytes 1572872 | tf_op jit(solution)/shard_map/ppermute | solution.py:14
  100.4 12.2 %all-to-all-start.5 = ((bf16[256,8,128]{2,1,0:T(8,128)(2,1)}), bf16[256,8,128]{2,1,0:T(8,128)(2,1)S(1)}, u32[]{:S(2)}, u32[]{:S(2)}) async-start(bf16[256,8,128]{2,1,0:T(8,128)(2,1)} %copy.60), calls=%async_computation.5 | async-start | bytes 1048576 | tf_op jit(solution)/shard_map/all_to_all | solution.py:107
  105.1 24.1 %collective-permute-start.9 = (bf16[256,8,128]{2,0,1:T(8,128)(2,1)}, bf16[256,8,128]{2,0,1:T(8,128)(2,1)S(1)}, u32[]{:S(2)}, u32[]{:S(2)}) collective-permute-start(bf16[256,8,128]{2,0,1:T(8,128)(2,1)} %get-tuple-element.4), channel_id=1, source_target_pairs={{2,0},{4,2},{6,4},{8,6},{10,8},{12,10},{14,12},{16,14},{18,16},{20... | collective-permute-start | bytes 1572872 | tf_op jit(solution)/shard_map/ppermute | solution.py:14
  107.1 22.0 %collective-permute-start.11 = (bf16[256,8,128]{2,0,1:T(8,128)(2,1)}, bf16[256,8,128]{2,0,1:T(8,128)(2,1)S(1)}, u32[]{:S(2)}, u32[]{:S(2)}) collective-permute-start(bf16[256,8,128]{2,0,1:T(8,128)(2,1)} %get-tuple-element.5), channel_id=1, source_target_pairs={{6,0},{8,2},{10,4},{12,6},{14,8},{16,10},{18,12},{20,14},{22,16},{... | collective-permute-start | bytes 1572872 | tf_op jit(solution)/shard_map/ppermute | solution.py:14
  109.1 37.8 %collective-permute-start.10 = (bf16[256,8,128]{2,0,1:T(8,128)(2,1)}, bf16[256,8,128]{2,0,1:T(8,128)(2,1)}, u32[]{:S(2)}, u32[]{:S(2)}) collective-permute-start(bf16[256,8,128]{2,0,1:T(8,128)(2,1)} %get-tuple-element.6), channel_id=1, source_target_pairs={{4,0},{6,2},{8,4},{10,6},{12,8},{14,10},{16,12},{18,14},{20,16},{2... | collective-permute-start | bytes 1572872 | tf_op jit(solution)/shard_map/ppermute | solution.py:14
  112.6 13.1 %all-to-all-start.3 = ((bf16[256,8,128]{2,1,0:T(8,128)(2,1)}), bf16[256,8,128]{2,1,0:T(8,128)(2,1)S(1)}, u32[]{:S(2)}, u32[]{:S(2)}) async-start(bf16[256,8,128]{2,1,0:T(8,128)(2,1)} %copy.52), calls=%async_computation.3 | async-start | bytes 1048576 | tf_op jit(solution)/shard_map/all_to_all | solution.py:106
  125.7 24.2 %all-to-all-start.6 = ((bf16[256,8,128]{2,1,0:T(8,128)(2,1)}), bf16[256,8,128]{2,1,0:T(8,128)(2,1)S(1)}, u32[]{:S(2)}, u32[]{:S(2)}) async-start(bf16[256,8,128]{2,1,0:T(8,128)(2,1)} %copy.62), calls=%async_computation.6 | async-start | bytes 1048576 | tf_op jit(solution)/shard_map/all_to_all | solution.py:108
  129.2 17.7 %copy-start.5 = (bf16[256,8,128]{2,0,1:T(8,128)(2,1)}, bf16[256,8,128]{2,0,1:T(8,128)(2,1)S(1)}, u32[]{:S(2)}) copy-start(bf16[256,8,128]{2,0,1:T(8,128)(2,1)S(1)} %collective-permute-done.11) | copy-start | bytes 1572868
  149.8 10.1 %all-to-all-start.7 = ((bf16[256,8,128]{2,1,0:T(8,128)(2,1)}), bf16[256,8,128]{2,1,0:T(8,128)(2,1)S(1)}, u32[]{:S(2)}, u32[]{:S(2)}) async-start(bf16[256,8,128]{2,1,0:T(8,128)(2,1)} %copy.65), calls=%async_computation.7 | async-start | bytes 1048576 | tf_op jit(solution)/shard_map/all_to_all | solution.py:111
where the time goes:
time: 162 us; the launch traced here: 161 us
  starting transfers between devices  49.6 us (31%)
  waiting for transfers between devices  38.7 us (24%)
  blocking collectives  22 us (14%)
  local copies, waits for them, and re-layouts  21.2 us (13%)
  matrix products  19.7 us (12%)
  other arithmetic  8.54 us (5%)
    ppermute x12, starting transfers between devices, from_behind(): return lax.ppermute(block, axis, route)  28.6 us
    ppermute x12, waiting for transfers between devices, from_behind(): return lax.ppermute(block, axis, route)  24.2 us
    all_to_all x1, blocking collectives, local(): lax.all_to_all(values, 'head', split_axis=1, concat_axis=0, tiled=True)  11.2 us
    all_to_all x1, blocking collectives, local(): lax.all_to_all(keys, 'head', split_axis=1, concat_axis=0, tiled=True)  10.8 us
    sub x1, matrix products, attend(): weights = jnp.exp(scores - highest)  7.57 us
    unnamed x25, local copies, waits for them, and re-layouts  7.25 us
    all_to_all x1, waiting for transfers between devices, local(): lax.all_to_all(queries, 'head', split_axis=1, concat_axis=0, tiled=True)  5.35 us
    all_to_all x1, waiting for transfers between devices, local(): lax.all_to_all(out_grad, 'head', split_axis=1, concat_axis=0, tiled=True)  4.71 us
  transfers between devices with their start and end apart: 18, of which 6 were waited for; matrix products, arithmetic and copies ran while one was open for 24% of the time, Pallas kernels for 0%

commit v1 on v0

v1 whole, which is shorter than its diff:
```python
import functools
import math

import jax
import jax.numpy as jnp
from jax import lax
from jax.experimental import pallas as pl
from jax.experimental.pallas import tpu as pltpu
from jax.sharding import PartitionSpec as P

R = 3
MESH = pl.DeviceIdType.MESH
BF16, F32 = jnp.bfloat16, jnp.float32


def dot(a, b, ca, cb):
    return lax.dot_general(a, b, (((ca,), (cb,)), ((), ())), preferred_element_type=F32)


def kernel(
    nctx, nhead, chunks, lists_ref, x_ref, out_ref,
    blk, near, mid, far, p1, p2, p3, bud, ra, rb, own, outb,
    s_loc, s_yin, r_yin, s_ctx, r_ctx, s_gr, r_gr, s_out, r_out, s_oloc,
):
    ctx = lax.axis_index("ctx")
    head = lax.axis_index("head")
    heads = blk.shape[2]
    length = blk.shape[3]
    width = blk.shape[4]
    rows = length // nhead
    held = heads * chunks
    even = lax.rem(ctx, 2) == 0
    odd = lax.rem(ctx, 2) == 1
    buddy = ctx + 1 - 2 * lax.rem(ctx, 2)
    score_scale = 1.0 / math.sqrt(width)
    mine = pl.ds(pl.multiple_of(head * rows, rows), rows)

    def mate(step):
        return lax.rem(head + step, nhead)

    barrier = pltpu.get_barrier_semaphore()
    for step in range(1, nhead):
        pl.semaphore_signal(barrier, inc=1, device_id=(ctx, mate(step)), device_id_type=MESH)
    near_by = 0
    for away in (-3, -1, 1, 3):
        other = ctx + away
        inside = (other >= 0) & (other < nctx)

        @pl.when(inside)
        def _():
            pl.semaphore_signal(barrier, inc=1, device_id=(other, head), device_id_type=MESH)

        near_by = near_by + inside.astype(jnp.int32)
    pl.semaphore_wait(barrier, near_by + (nhead - 1))

    def yin_out(j, kind, step):
        to = mate(step)
        return pltpu.make_async_remote_copy(
            src_ref=x_ref.at[pl.ds(2 * kind, 2), pl.ds(to * held + j * heads, heads)],
            dst_ref=blk.at[j, pl.ds(2 * kind, 2), :, mine],
            send_sem=s_yin.at[j, kind, step - 1],
            recv_sem=r_yin.at[j, kind, step - 1],
            device_id=(ctx, to),
            device_id_type=MESH,
        )

    def yin_in(j, kind, step):
        source = lax.rem(head + nhead - step, nhead)
        theirs = pl.ds(pl.multiple_of(source * rows, rows), rows)
        return pltpu.make_async_remote_copy(
            src_ref=x_ref.at[pl.ds(2 * kind, 2), pl.ds(j * heads, heads)],
            dst_ref=blk.at[j, pl.ds(2 * kind, 2), :, theirs],
            send_sem=s_yin.at[j, kind, step - 1],
            recv_sem=r_yin.at[j, kind, step - 1],
            device_id=(ctx, source),
            device_id_type=MESH,
        )

    def yin_local(j, kind):
        return pltpu.make_async_copy(
            x_ref.at[pl.ds(2 * kind, 2), pl.ds(head * held + j * heads, heads)],
            blk.at[j, pl.ds(2 * kind, 2), :, mine],
            s_loc.at[j, kind],
        )

    def yin_start(j, kind):
        for step in range(1, nhead):
            yin_out(j, kind, step).start()
        yin_local(j, kind).start()

    def yin_wait(j, kind):
        for step in range(1, nhead):
            yin_in(j, kind, step).wait_recv()
        yin_local(j, kind).wait()

    def ctx_copy(src, dst, sems, recvs, j, which, to):
        return pltpu.make_async_remote_copy(
            src_ref=src,
            dst_ref=dst,
            send_sem=sems.at[j, which],
            recv_sem=recvs.at[j, which],
            device_id=(to, head),
            device_id_type=MESH,
        )

    def kv(j):
        return blk.at[j, pl.ds(0, 2)]

    def send_near(j):
        return ctx_copy(kv(j), near.at[j], s_ctx, r_ctx, j, 0, ctx + 1)

    def send_far(j):
        return ctx_copy(kv(j), far.at[j], s_ctx, r_ctx, j, 1, ctx + 3)

    def pass_near(j):
        return ctx_copy(near.at[j], mid.at[j], s_ctx, r_ctx, j, 2, buddy)

    def pass_far(j):
        return ctx_copy(far.at[j], mid.at[j], s_ctx, r_ctx, j, 2, buddy)

    def give_mid(j):
        return ctx_copy(p2.at[j], bud.at[j], s_gr, r_gr, j, 0, buddy)

    def give_near(j):
        return ctx_copy(p1.at[j], ra.at[j], s_gr, r_gr, j, 1, ctx - 1)

    def give_far(j):
        return ctx_copy(p3.at[j], rb.at[j], s_gr, r_gr, j, 2, ctx - 3)

    has1, has3 = ctx >= 1, ctx >= 3
    to1, to3 = ctx + 1 < nctx, ctx + 3 < nctx
    pass1 = even & has1
    pass3 = odd & has3
    mid_in = ctx >= 2
    bud_in = (even & has1) | (odd & has3)

    def yout_out(j, kind, step):
        to = mate(step)
        part = pl.ds(pl.multiple_of(to * rows, rows), rows)
        return pltpu.make_async_remote_copy(
            src_ref=outb.at[j, pl.ds(2 * kind, 2), :, part],
            dst_ref=out_ref.at[pl.ds(2 * kind, 2), pl.ds(head * held + j * heads, heads)],
            send_sem=s_out.at[j, kind, step - 1],
            recv_sem=r_out.at[j, kind, step - 1],
            device_id=(ctx, to),
            device_id_type=MESH,
        )

    def yout_in(j, kind, step):
        source = lax.rem(head + nhead - step, nhead)
        return pltpu.make_async_remote_copy(
            src_ref=outb.at[j, pl.ds(2 * kind, 2), :, mine],
            dst_ref=out_ref.at[pl.ds(2 * kind, 2), pl.ds(source * held + j * heads, heads)],
            send_sem=s_out.at[j, kind, step - 1],
            recv_sem=r_out.at[j, kind, step - 1],
            device_id=(ctx, source),
            device_id_type=MESH,
        )

    def yout_local(j, kind):
        return pltpu.make_async_copy(
            outb.at[j, pl.ds(2 * kind, 2), :, mine],
            out_ref.at[pl.ds(2 * kind, 2), pl.ds(head * held + j * heads, heads)],
            s_oloc.at[j, kind],
        )

    def yout_start(j, kind):
        for step in range(1, nhead):
            yout_out(j, kind, step).start()
        yout_local(j, kind).start()

    addend = []
    for distance in range(1, R + 1):
        block = ctx - distance
        listed = block == lists_ref[0, 0]
        for entry in range(1, lists_ref.shape[1]):
            listed = listed | (block == lists_ref[0, entry])
        addend.append(jnp.where(listed & (block >= 0), jnp.float32(0), jnp.float32(-jnp.inf)))

    def attend(j, h):
        key0, value0 = blk[j, 0, h], blk[j, 1, h]
        query, grad = blk[j, 2, h], blk[j, 3, h]
        windows = (near, mid, far)
        keys = [key0] + [w[j, 0, h] for w in windows]
        values = [value0] + [w[j, 1, h] for w in windows]
        scores = [dot(k, query, 1, 1) for k in keys]
        s_ids = lax.broadcasted_iota(jnp.int32, (length, length), 0)
        t_ids = lax.broadcasted_iota(jnp.int32, (length, length), 1)
        scores[0] = jnp.where(s_ids <= t_ids, scores[0], -jnp.inf)
        for d in range(1, R + 1):
            scores[d] = scores[d] + addend[d - 1]
        highest = functools.reduce(
            jnp.maximum, [jnp.max(s, axis=0, keepdims=True) for s in scores]
        )
        to_exp2 = score_scale * math.log2(math.e)
        weights = [jnp.exp2((s - highest) * to_exp2) for s in scores]
        total = functools.reduce(
            jnp.add, [jnp.sum(w, axis=0, keepdims=True) for w in weights]
        )
        inverse = 1.0 / total
        probs = [w * inverse for w in weights]
        low = [p.astype(BF16) for p in probs]
        attended = functools.reduce(
            jnp.add, [dot(p, v, 0, 0) for p, v in zip(low, values)]
        ).astype(BF16)
        outb[j, 0, h] = attended
        product = grad.astype(F32) * attended.astype(F32)
        centre = jnp.sum(product.T, axis=0, keepdims=True)
        slopes = [
            (p * (dot(v, grad, 1, 1) - centre)).astype(BF16) for p, v in zip(probs, values)
        ]
        grad_query = functools.reduce(
            jnp.add, [dot(g, k, 0, 0) for g, k in zip(slopes, keys)]
        )
        outb[j, 1, h] = (grad_query * score_scale).astype(BF16)
        for d, slot in enumerate((own, p1, p2, p3)):
            slot[j, 0, h] = (dot(slopes[d], query, 1, 0) * score_scale).astype(slot.dtype)
            slot[j, 1, h] = dot(low[d], grad, 1, 0).astype(slot.dtype)

    order = [(0, 0)]
    for j in range(chunks):
        if j + 1 < chunks:
            order.append((j + 1, 0))
        order.append((j, 1))
    for j, kind in order:
        yin_start(j, kind)
    for distance, slot in ((1, near), (2, mid), (3, far)):

        @pl.when(ctx < distance)
        def _():
            slot[...] = jnp.zeros_like(slot)

    def stage(t, lag, run):
        @pl.when((t >= lag) & (t < lag + chunks))
        def _():
            run(t - lag)

    def forward(j):
        yin_wait(j, 0)
        pl.when(to3)(lambda: send_far(j).start())
        pl.when(to1)(lambda: send_near(j).start())

    def relay(j):
        pl.when(has3)(lambda: send_far(j).wait_recv())
        pl.when(pass3)(lambda: pass_far(j).start())
        pl.when(has1)(lambda: send_near(j).wait_recv())
        pl.when(pass1)(lambda: pass_near(j).start())

    def compute(j):
        yin_wait(j, 1)
        pl.when(mid_in)(lambda: pass_near(j).wait_recv())

        def one(h, carry):
            attend(j, h)
            return carry

        lax.fori_loop(0, heads, one, 0)
        pl.when(mid_in)(lambda: give_mid(j).start())
        pl.when(even & has3)(lambda: give_far(j).start())
        pl.when(odd)(lambda: give_near(j).start())
        yout_start(j, 0)

    def combine(j):
        pl.when(bud_in)(lambda: give_mid(j).wait_recv())

        @pl.when(pass1)
        def _():
            p1[j] = (p1[j].astype(F32) + bud[j].astype(F32)).astype(BF16)
            give_near(j).start()

        @pl.when(pass3)
        def _():
            p3[j] = (p3[j].astype(F32) + bud[j].astype(F32)).astype(BF16)
            give_far(j).start()

    def finish(j):
        @pl.when(to1)
        def _():
            give_near(j).wait_recv()
            own[j] = own[j] + ra[j].astype(F32)

        @pl.when(to3)
        def _():
            give_far(j).wait_recv()
            own[j] = own[j] + rb[j].astype(F32)

        outb[j, pl.ds(2, 2)] = own[j].astype(BF16)
        yout_start(j, 1)

    def body(t, carry):
        stage(t, 0, forward)
        stage(t, 1, relay)
        stage(t, 2, compute)
        stage(t, 3, combine)
        stage(t, 4, finish)
        return carry

    lax.fori_loop(0, chunks + 4, body, 0)

    def drain(j, carry):
        for kind in range(2):
            for step in range(1, nhead):
                yin_out(j, kind, step).wait_send()
                yout_out(j, kind, step).wait_send()
                yout_in(j, kind, step).wait_recv()
            yout_local(j, kind).wait()
        pl.when(to1)(lambda: send_near(j).wait_send())
        pl.when(to3)(lambda: send_far(j).wait_send())
        pl.when(pass1)(lambda: pass_near(j).wait_send())
        pl.when(pass3)(lambda: pass_far(j).wait_send())
        pl.when(mid_in)(lambda: give_mid(j).wait_send())
        pl.when(has1)(lambda: give_near(j).wait_send())
        pl.when(has3)(lambda: give_far(j).wait_send())
        return carry

    lax.fori_loop(0, chunks, drain, 0)


def local(nctx, nhead, queries, keys, values, out_grad, block_lists):
    rows, heads_all, width = queries.shape
    length = rows * nhead
    held = heads_all // nhead
    chunks = 4
    heads = held // chunks
    stacked = jnp.stack([a.transpose(1, 0, 2) for a in (keys, values, queries, out_grad)])
    half = pltpu.VMEM((chunks, 2, heads, length, width), BF16)
    dma = pltpu.SemaphoreType.DMA
    flops = 6 * 2 * held * length * length * (R + 1) * width
    out = pl.pallas_call(
        functools.partial(kernel, nctx, nhead, chunks),
        out_shape=jax.ShapeDtypeStruct((4, heads_all, rows, width), BF16),
        in_specs=[
            pl.BlockSpec(memory_space=pltpu.SMEM),
            pl.BlockSpec(memory_space=pl.ANY),
        ],
        out_specs=pl.BlockSpec(memory_space=pl.ANY),
        scratch_shapes=[
            pltpu.VMEM((chunks, 4, heads, length, width), BF16),
            half, half, half,
            half, half, half,
            half, half, half,
            pltpu.VMEM((chunks, 2, heads, length, width), F32),
            pltpu.VMEM((chunks, 4, heads, length, width), BF16),
            dma((chunks, 2)),
            dma((chunks, 2, nhead - 1)),
            dma((chunks, 2, nhead - 1)),
            dma((chunks, 3)),
            dma((chunks, 3)),
            dma((chunks, 3)),
            dma((chunks, 3)),
            dma((chunks, 2, nhead - 1)),
            dma((chunks, 2, nhead - 1)),
            dma((chunks, 2)),
        ],
        compiler_params=pltpu.CompilerParams(
            collective_id=0, has_side_effects=True, vmem_limit_bytes=48 * 1024 * 1024
        ),
        cost_estimate=pl.CostEstimate(
            flops=flops, bytes_accessed=16 * rows * heads_all * width, transcendentals=0
        ),
    )(block_lists, stacked)
    return tuple(out[a].transpose(1, 0, 2) for a in range(4))


def solution(mesh):
    split = P(("ctx", "head"), None, None)
    return jax.shard_map(
        functools.partial(local, mesh.shape["ctx"], mesh.shape["head"]),
        mesh=mesh,
        in_specs=(split, split, split, split, P("ctx", None)),
        out_specs=(split, split, split, split),
        check_vma=False,
    )
```

time: 162 us -> 83.8 us (0.52)
  the two profiles are of different devices: /device:TPU:10 before, /device:TPU:23 now
where the time goes in v1:
time: 83.8 us; the launch traced here: 83.7 us
  Pallas kernels  75.8 us (90%)
  local copies, waits for them, and re-layouts  6.89 us (8%)
    pallas_call x1, Pallas kernels, local(): pl.pallas_call(functools.partial(kernel, nctx, nhead, chunks), out_shape=...  75.8 us
    unnamed x10, local copies, waits for them, and re-layouts  4.92 us
    another operation x2, local copies, waits for them, and re-layouts, local(): jnp.stack([a.transpose(1, 0, 2) for a in (keys, values, queries, out_grad)])  1.83 us

profile of v1, /device:TPU:23, one launch (start us, length us, event | category | flops | bytes accessed | tf_op | source)
XLA Modules:
  0.0 83.7 jit_solution(1344971372870784778)
XLA Ops:
  0.6 0.0 copy-start.1
  0.6 0.0 copy-start.2
  0.7 1.6 %copy_bitcast_fusion = (bf16[1,16,128,128]{3,2,1,0:T(8,128)(2,1)S(1)}, bf16[1,16,128,128]{3,2,1,0:T(8,128)(2,1)S(1)}) fusion(bf16[128,16,128]{2,1,0:T(8,128)(2,1)} %param.8, bf16[128,16,128]{2,1,0:T(8,128)(2,1)} %param.5), kind=kLoop, calls=%fused_computation.1 | loop fusion | bytes 2097152 | tf_op jit(solution)/shard_map/stack | solution.py:325
  2.2 0.0 copy-done.1
  2.2 0.0 copy-done.2
  2.2 0.3 copy_bitcast_fusion.2
  2.5 0.0 copy-start
  2.5 0.3 pad_maximum_fusion.x_ref
  2.8 0.4 copy-done
  3.2 75.8 %shard_map.84 = bf16[4,16,128,128]{3,2,1,0:T(8,128)(2,1)S(1)} custom-call(s32[1,3]{1,0:T(1,128)S(1)} %copy-done, bf16[4,16,128,128]{3,2,1,0:T(8,128)(2,1)S(1)} %pad_maximum_fusion.x_ref), custom_call_target="tpu_custom_call" | custom-call | flops 3221225472 | bytes 4194304 | tf_op jit(solution)/shard_map/pallas_call | solution.py:329
  79.0 0.1 slice_bitcast_fusion
  79.1 1.1 %copy.16 = bf16[128,16,128]{2,1,0:T(8,128)(2,1)} copy(bf16[128,16,128]{2,0,1:T(8,128)(2,1)S(1)} %get-tuple-element.8) | data formatting | bytes 1048576
  80.3 1.1 %copy.15 = bf16[128,16,128]{2,1,0:T(8,128)(2,1)} copy(bf16[128,16,128]{2,0,1:T(8,128)(2,1)S(1)} %get-tuple-element.9) | data formatting | bytes 1048576
  81.4 1.1 %copy.14 = bf16[128,16,128]{2,1,0:T(8,128)(2,1)} copy(bf16[128,16,128]{2,0,1:T(8,128)(2,1)S(1)} %get-tuple-element.10) | data formatting | bytes 1048576
  82.5 1.1 %copy.13 = bf16[128,16,128]{2,1,0:T(8,128)(2,1)} copy(bf16[128,16,128]{2,0,1:T(8,128)(2,1)S(1)} %get-tuple-element.11) | data formatting | bytes 1048576
Async XLA Ops:
  0.6 1.6 %copy-start.1 = (bf16[128,16,128]{2,1,0:T(8,128)(2,1)S(1)}, bf16[128,16,128]{2,1,0:T(8,128)(2,1)}, u32[]{:S(2)}) copy-start(bf16[128,16,128]{2,1,0:T(8,128)(2,1)} %param.7) | copy-start | bytes 1572868
  0.6 1.6 %copy-start.2 = (bf16[128,16,128]{2,1,0:T(8,128)(2,1)S(1)}, bf16[128,16,128]{2,1,0:T(8,128)(2,1)}, u32[]{:S(2)}) copy-start(bf16[128,16,128]{2,1,0:T(8,128)(2,1)} %param.6) | copy-start | bytes 1572868
  2.5 0.7 copy-start

commit v2 on v1

--- a/solution.py
+++ b/solution.py
@@ -19,7 +19,7 @@
 
 def kernel(
     nctx, nhead, chunks, lists_ref, x_ref, out_ref,
-    blk, near, mid, far, p1, p2, p3, bud, ra, rb, own, outb,
+    blk, near, mid, far, p1, p2, p3, bud, hop, ra, rb, own, outb,
     s_loc, s_yin, r_yin, s_ctx, r_ctx, s_gr, r_gr, s_out, r_out, s_oloc,
 ):
     ctx = lax.axis_index("ctx")
@@ -31,6 +31,7 @@
     held = heads * chunks
     even = lax.rem(ctx, 2) == 0
     odd = lax.rem(ctx, 2) == 1
+    place = lax.rem(ctx, 4)
     buddy = ctx + 1 - 2 * lax.rem(ctx, 2)
     score_scale = 1.0 / math.sqrt(width)
     mine = pl.ds(pl.multiple_of(head * rows, rows), rows)
@@ -51,6 +52,15 @@
             pl.semaphore_signal(barrier, inc=1, device_id=(other, head), device_id_type=MESH)
 
         near_by = near_by + inside.astype(jnp.int32)
+    first, third, last = place == 0, place == 2, place == 3
+    has1, has3 = ctx >= 1, ctx >= 3
+    for role, other in ((third & has3, ctx - 2), (first & has1, ctx + 2)):
+
+        @pl.when(role)
+        def _():
+            pl.semaphore_signal(barrier, inc=1, device_id=(other, head), device_id_type=MESH)
+
+        near_by = near_by + role.astype(jnp.int32)
     pl.semaphore_wait(barrier, near_by + (nhead - 1))
 
     def yin_out(j, kind, step):
@@ -93,12 +103,12 @@
             yin_in(j, kind, step).wait_recv()
         yin_local(j, kind).wait()
 
-    def ctx_copy(src, dst, sems, recvs, j, which, to):
+    def ctx_copy(src, dst, sems, recvs, j, which, to, lands=None):
         return pltpu.make_async_remote_copy(
             src_ref=src,
             dst_ref=dst,
             send_sem=sems.at[j, which],
-            recv_sem=recvs.at[j, which],
+            recv_sem=recvs.at[j, which if lands is None else lands],
             device_id=(to, head),
             device_id_type=MESH,
         )
@@ -118,6 +128,12 @@
     def pass_far(j):
         return ctx_copy(far.at[j], mid.at[j], s_ctx, r_ctx, j, 2, buddy)
 
+    def hop_near(j):
+        return ctx_copy(far.at[j], near.at[j], s_ctx, r_ctx, j, 3, ctx - 2, 0)
+
+    def hop_back(j):
+        return ctx_copy(p1.at[j], hop.at[j], s_gr, r_gr, j, 3, ctx + 2)
+
     def give_mid(j):
         return ctx_copy(p2.at[j], bud.at[j], s_gr, r_gr, j, 0, buddy)
 
@@ -127,8 +143,8 @@
     def give_far(j):
         return ctx_copy(p3.at[j], rb.at[j], s_gr, r_gr, j, 2, ctx - 3)
 
-    has1, has3 = ctx >= 1, ctx >= 3
-    to1, to3 = ctx + 1 < nctx, ctx + 3 < nctx
+    to1, to3 = (ctx + 1 < nctx) & ~last, ctx + 3 < nctx
+    hop1, hop3 = first & has1, third & has3
     pass1 = even & has1
     pass3 = odd & has3
     mid_in = ctx >= 2
@@ -242,9 +258,16 @@
 
     def relay(j):
         pl.when(has3)(lambda: send_far(j).wait_recv())
+        pl.when(hop3)(lambda: hop_near(j).start())
         pl.when(pass3)(lambda: pass_far(j).start())
-        pl.when(has1)(lambda: send_near(j).wait_recv())
-        pl.when(pass1)(lambda: pass_near(j).start())
+        pl.when(has1 & ~first)(lambda: send_near(j).wait_recv())
+        pl.when(third)(lambda: pass_near(j).start())
+
+    def relay_again(j):
+        @pl.when(hop1)
+        def _():
+            send_near(j).wait_recv()
+            pass_near(j).start()
 
     def compute(j):
         yin_wait(j, 1)
@@ -256,7 +279,7 @@
 
         lax.fori_loop(0, heads, one, 0)
         pl.when(mid_in)(lambda: give_mid(j).start())
-        pl.when(even & has3)(lambda: give_far(j).start())
+        pl.when(hop1)(lambda: give_far(j).start())
         pl.when(odd)(lambda: give_near(j).start())
         yout_start(j, 0)
 
@@ -266,11 +289,19 @@
         @pl.when(pass1)
         def _():
             p1[j] = (p1[j].astype(F32) + bud[j].astype(F32)).astype(BF16)
-            give_near(j).start()
+            pl.when(third)(lambda: give_near(j).start())
+            pl.when(first)(lambda: hop_back(j).start())
 
         @pl.when(pass3)
         def _():
             p3[j] = (p3[j].astype(F32) + bud[j].astype(F32)).astype(BF16)
+            give_far(j).start()
+
+    def combine_again(j):
+        @pl.when(hop3)
+        def _():
+            hop_back(j).wait_recv()
+            p3[j] = (p3[j].astype(F32) + hop[j].astype(F32)).astype(BF16)
             give_far(j).start()
 
     def finish(j):
@@ -290,12 +321,14 @@
     def body(t, carry):
         stage(t, 0, forward)
         stage(t, 1, relay)
-        stage(t, 2, compute)
-        stage(t, 3, combine)
-        stage(t, 4, finish)
+        stage(t, 3, relay_again)
+        stage(t, 4, compute)
+        stage(t, 5, combine)
+        stage(t, 6, combine_again)
+        stage(t, 8, finish)
         return carry
 
-    lax.fori_loop(0, chunks + 4, body, 0)
+    lax.fori_loop(0, chunks + 8, body, 0)
 
     def drain(j, carry):
         for kind in range(2):
@@ -309,7 +342,9 @@
         pl.when(pass1)(lambda: pass_near(j).wait_send())
         pl.when(pass3)(lambda: pass_far(j).wait_send())
         pl.when(mid_in)(lambda: give_mid(j).wait_send())
-        pl.when(has1)(lambda: give_near(j).wait_send())
+        pl.when(hop3)(lambda: hop_near(j).wait_send())
+        pl.when(hop1)(lambda: hop_back(j).wait_send())
+        pl.when(has1 & ~first)(lambda: give_near(j).wait_send())
         pl.when(has3)(lambda: give_far(j).wait_send())
         return carry
 
@@ -320,7 +355,7 @@
     rows, heads_all, width = queries.shape
     length = rows * nhead
     held = heads_all // nhead
-    chunks = 4
+    chunks = 8
     heads = held // chunks
     stacked = jnp.stack([a.transpose(1, 0, 2) for a in (keys, values, queries, out_grad)])
     half = pltpu.VMEM((chunks, 2, heads, length, width), BF16)
@@ -338,16 +373,16 @@
             pltpu.VMEM((chunks, 4, heads, length, width), BF16),
             half, half, half,
             half, half, half,
-            half, half, half,
+            half, half, half, half,
             pltpu.VMEM((chunks, 2, heads, length, width), F32),
             pltpu.VMEM((chunks, 4, heads, length, width), BF16),
             dma((chunks, 2)),
             dma((chunks, 2, nhead - 1)),
             dma((chunks, 2, nhead - 1)),
+            dma((chunks, 4)),
             dma((chunks, 3)),
-            dma((chunks, 3)),
-            dma((chunks, 3)),
-            dma((chunks, 3)),
+            dma((chunks, 4)),
+            dma((chunks, 4)),
             dma((chunks, 2, nhead - 1)),
             dma((chunks, 2, nhead - 1)),
             dma((chunks, 2)),

time: 83.8 us -> 71 us (0.85)
  Pallas kernels: 75.8 us -> 63 us
    pallas_call x1, Pallas kernels: 75.8 us -> 63 us  [local(): pl.pallas_call(functools.partial(kernel, nctx, nhead, chunks), out_shape=...]
where the time goes in v2:
time: 71 us; the launch traced here: 70.9 us
  Pallas kernels  63 us (89%)
  local copies, waits for them, and re-layouts  6.89 us (10%)
  between operations  0.71 us (1%)
    pallas_call x1, Pallas kernels, local(): pl.pallas_call(functools.partial(kernel, nctx, nhead, chunks), out_shape=...  63 us
    unnamed x10, local copies, waits for them, and re-layouts  4.92 us
    another operation x2, local copies, waits for them, and re-layouts, local(): jnp.stack([a.transpose(1, 0, 2) for a in (keys, values, queries, out_grad)])  1.83 us

profile of v2, /device:TPU:23, one launch (start us, length us, event | category | flops | bytes accessed | tf_op | source)
XLA Modules:
  0.0 70.9 jit_solution(17350726020280033265)
XLA Ops:
  0.6 0.0 copy-start.1
  0.6 0.0 copy-start.2
  0.7 1.6 %copy_bitcast_fusion = (bf16[1,16,128,128]{3,2,1,0:T(8,128)(2,1)S(1)}, bf16[1,16,128,128]{3,2,1,0:T(8,128)(2,1)S(1)}) fusion(bf16[128,16,128]{2,1,0:T(8,128)(2,1)} %param.8, bf16[128,16,128]{2,1,0:T(8,128)(2,1)} %param.5), kind=kLoop, calls=%fused_computation.1 | loop fusion | bytes 2097152 | tf_op jit(solution)/shard_map/stack | solution.py:360
  2.2 0.0 copy-done.1
  2.2 0.0 copy-done.2
  2.2 0.3 copy_bitcast_fusion.2
  2.5 0.0 copy-start
  2.5 0.3 pad_maximum_fusion.x_ref
  2.8 0.4 copy-done
  3.2 63.0 %shard_map.84 = bf16[4,16,128,128]{3,2,1,0:T(8,128)(2,1)S(1)} custom-call(s32[1,3]{1,0:T(1,128)S(1)} %copy-done, bf16[4,16,128,128]{3,2,1,0:T(8,128)(2,1)S(1)} %pad_maximum_fusion.x_ref), custom_call_target="tpu_custom_call" | custom-call | flops 3221225472 | bytes 4194304 | tf_op jit(solution)/shard_map/pallas_call | solution.py:364
  66.2 0.1 slice_bitcast_fusion
  66.3 1.1 %copy.16 = bf16[128,16,128]{2,1,0:T(8,128)(2,1)} copy(bf16[128,16,128]{2,0,1:T(8,128)(2,1)S(1)} %get-tuple-element.8) | data formatting | bytes 1048576
  67.5 1.1 %copy.15 = bf16[128,16,128]{2,1,0:T(8,128)(2,1)} copy(bf16[128,16,128]{2,0,1:T(8,128)(2,1)S(1)} %get-tuple-element.9) | data formatting | bytes 1048576
  68.6 1.1 %copy.14 = bf16[128,16,128]{2,1,0:T(8,128)(2,1)} copy(bf16[128,16,128]{2,0,1:T(8,128)(2,1)S(1)} %get-tuple-element.10) | data formatting | bytes 1048576
  69.7 1.1 %copy.13 = bf16[128,16,128]{2,1,0:T(8,128)(2,1)} copy(bf16[128,16,128]{2,0,1:T(8,128)(2,1)S(1)} %get-tuple-element.11) | data formatting | bytes 1048576
Async XLA Ops:
  0.6 1.6 %copy-start.1 = (bf16[128,16,128]{2,1,0:T(8,128)(2,1)S(1)}, bf16[128,16,128]{2,1,0:T(8,128)(2,1)}, u32[]{:S(2)}) copy-start(bf16[128,16,128]{2,1,0:T(8,128)(2,1)} %param.7) | copy-start | bytes 1572868
  0.6 1.6 %copy-start.2 = (bf16[128,16,128]{2,1,0:T(8,128)(2,1)S(1)}, bf16[128,16,128]{2,1,0:T(8,128)(2,1)}, u32[]{:S(2)}) copy-start(bf16[128,16,128]{2,1,0:T(8,128)(2,1)} %param.6) | copy-start | bytes 1572868
  2.5 0.7 copy-start

commit v3 on v2

--- a/solution.py
+++ b/solution.py
@@ -18,8 +18,8 @@
 
 
 def kernel(
-    nctx, nhead, chunks, lists_ref, x_ref, out_ref,
-    blk, near, mid, far, p1, p2, p3, bud, hop, ra, rb, own, outb,
+    nctx, nhead, chunks, lists_ref, x_ref, out0, out1, out2, out3,
+    out_ref, blk, near, mid, far, p1, p2, p3, bud, hop, ra, rb, own, outb,
     s_loc, s_yin, r_yin, s_ctx, r_ctx, s_gr, r_gr, s_out, r_out, s_oloc,
 ):
     ctx = lax.axis_index("ctx")
@@ -318,25 +318,45 @@
         outb[j, pl.ds(2, 2)] = own[j].astype(BF16)
         yout_start(j, 1)
 
+    group = 16
+
+    def settle(kind, results):
+        def landed(j, carry):
+            for step in range(1, nhead):
+                yout_in(j, kind, step).wait_recv()
+            yout_local(j, kind).wait()
+            return carry
+
+        lax.fori_loop(0, chunks, landed, 0)
+
+        def turn(n, carry):
+            some = pl.ds(pl.multiple_of(n * group, group), group)
+            for a, result in enumerate(results):
+                result[some] = jnp.swapaxes(out_ref[2 * kind + a, :, some, :], 0, 1)
+            return carry
+
+        lax.fori_loop(0, rows // group, turn, 0)
+
     def body(t, carry):
         stage(t, 0, forward)
         stage(t, 1, relay)
         stage(t, 3, relay_again)
-        stage(t, 4, compute)
-        stage(t, 5, combine)
-        stage(t, 6, combine_again)
-        stage(t, 8, finish)
+        stage(t, 5, compute)
+        stage(t, 6, combine)
+        stage(t, 7, combine_again)
+        pl.when(t == chunks + 8)(lambda: settle(0, (out0, out1)))
+        stage(t, 9, finish)
         return carry
 
-    lax.fori_loop(0, chunks + 8, body, 0)
+    lax.fori_loop(0, chunks + 9, body, 0)
+
+    settle(1, (out2, out3))
 
     def drain(j, carry):
         for kind in range(2):
             for step in range(1, nhead):
                 yin_out(j, kind, step).wait_send()
                 yout_out(j, kind, step).wait_send()
-                yout_in(j, kind, step).wait_recv()
-            yout_local(j, kind).wait()
         pl.when(to1)(lambda: send_near(j).wait_send())
         pl.when(to3)(lambda: send_far(j).wait_send())
         pl.when(pass1)(lambda: pass_near(j).wait_send())
@@ -363,13 +383,14 @@
     flops = 6 * 2 * held * length * length * (R + 1) * width
     out = pl.pallas_call(
         functools.partial(kernel, nctx, nhead, chunks),
-        out_shape=jax.ShapeDtypeStruct((4, heads_all, rows, width), BF16),
+        out_shape=[jax.ShapeDtypeStruct((rows, heads_all, width), BF16)] * 4,
         in_specs=[
             pl.BlockSpec(memory_space=pltpu.SMEM),
             pl.BlockSpec(memory_space=pl.ANY),
         ],
-        out_specs=pl.BlockSpec(memory_space=pl.ANY),
+        out_specs=[pl.BlockSpec(memory_space=pltpu.VMEM)] * 4,
         scratch_shapes=[
+            pltpu.VMEM((4, heads_all, rows, width), BF16),
             pltpu.VMEM((chunks, 4, heads, length, width), BF16),
             half, half, half,
             half, half, half,
@@ -394,7 +415,7 @@
             flops=flops, bytes_accessed=16 * rows * heads_all * width, transcendentals=0
         ),
     )(block_lists, stacked)
-    return tuple(out[a].transpose(1, 0, 2) for a in range(4))
+    return tuple(out)
 
 
 def solution(mesh):

time: 71 us -> 68.9 us (0.970); the launches traced: 70.9 us -> 67.7 us
  Pallas kernels: 63 us -> 61.3 us
  local copies, waits for them, and re-layouts: 6.89 us -> 5.39 us
    pallas_call x1, Pallas kernels: 63 us -> 61.3 us  [local(): pl.pallas_call(functools.partial(kernel, nctx, nhead, chunks), out_shape=...]
    unnamed x10, local copies, waits for them, and re-layouts: 4.92 us -> 3.56 us
where the time goes in v3:
time: 68.9 us; the launch traced here: 67.7 us
  Pallas kernels  61.3 us (89%)
  local copies, waits for them, and re-layouts  5.39 us (8%)
  between operations  0.7 us (1%)
    pallas_call x1, Pallas kernels, local(): pl.pallas_call(functools.partial(kernel, nctx, nhead, chunks), out_shape=...  61.3 us
    unnamed x10, local copies, waits for them, and re-layouts  3.56 us
    another operation x2, local copies, waits for them, and re-layouts, local(): jnp.stack([a.transpose(1, 0, 2) for a in (keys, values, queries, out_grad)])  1.83 us

profile of v3, /device:TPU:23, one launch (start us, length us, event | category | flops | bytes accessed | tf_op | source)
XLA Modules:
  0.0 67.7 jit_solution(14914418429871806938)
XLA Ops:
  0.6 0.0 copy-start.1
  0.6 0.0 copy-start.2
  0.7 1.6 %copy_bitcast_fusion = (bf16[1,16,128,128]{3,2,1,0:T(8,128)(2,1)S(1)}, bf16[1,16,128,128]{3,2,1,0:T(8,128)(2,1)S(1)}) fusion(bf16[128,16,128]{2,1,0:T(8,128)(2,1)} %param.8, bf16[128,16,128]{2,1,0:T(8,128)(2,1)} %param.5), kind=kLoop, calls=%fused_computation.1 | loop fusion | bytes 2097152 | tf_op jit(solution)/shard_map/stack | solution.py:380
  2.2 0.0 copy-done.1
  2.2 0.0 copy-done.2
  2.2 0.3 copy_bitcast_fusion.2
  2.5 0.0 copy-start
  2.5 0.3 pad_maximum_fusion.x_ref
  2.8 0.4 copy-done
  3.2 61.3 %shard_map.84 = (bf16[128,16,128]{2,1,0:T(8,128)(2,1)S(1)}, bf16[128,16,128]{2,1,0:T(8,128)(2,1)S(1)}, bf16[128,16,128]{2,1,0:T(8,128)(2,1)S(1)}, bf16[128,16,128]{2,1,0:T(8,128)(2,1)S(1)}) custom-call(s32[1,3]{1,0:T(1,128)S(1)} %copy-done, bf16[4,16,128,128]{3,2,1,0:T(8,128)(2,1)S(1)} %pad_maximum_fusion.x_ref), custom_call_target="tpu_custom_call" | custom-call | flops 3221225472 | bytes 4194304 | tf_op jit(solution)/shard_map/pallas_call | solution.py:384
  64.5 0.8 %copy.21 = bf16[128,16,128]{2,1,0:T(8,128)(2,1)} copy(bf16[128,16,128]{2,1,0:T(8,128)(2,1)S(1)} %get-tuple-element.12) | data formatting | bytes 1048576
  65.3 0.8 %copy.22 = bf16[128,16,128]{2,1,0:T(8,128)(2,1)} copy(bf16[128,16,128]{2,1,0:T(8,128)(2,1)S(1)} %get-tuple-element.13) | data formatting | bytes 1048576
  66.1 0.8 %copy.23 = bf16[128,16,128]{2,1,0:T(8,128)(2,1)} copy(bf16[128,16,128]{2,1,0:T(8,128)(2,1)S(1)} %get-tuple-element.14) | data formatting | bytes 1048576
  66.9 0.8 %copy.24 = bf16[128,16,128]{2,1,0:T(8,128)(2,1)} copy(bf16[128,16,128]{2,1,0:T(8,128)(2,1)S(1)} %get-tuple-element.15) | data formatting | bytes 1048576
Async XLA Ops:
  0.6 1.6 %copy-start.1 = (bf16[128,16,128]{2,1,0:T(8,128)(2,1)S(1)}, bf16[128,16,128]{2,1,0:T(8,128)(2,1)}, u32[]{:S(2)}) copy-start(bf16[128,16,128]{2,1,0:T(8,128)(2,1)} %param.7) | copy-start | bytes 1572868
  0.6 1.6 %copy-start.2 = (bf16[128,16,128]{2,1,0:T(8,128)(2,1)S(1)}, bf16[128,16,128]{2,1,0:T(8,128)(2,1)}, u32[]{:S(2)}) copy-start(bf16[128,16,128]{2,1,0:T(8,128)(2,1)} %param.6) | copy-start | bytes 1572868
  2.5 0.7 copy-start

commit v4 on v3

--- a/solution.py
+++ b/solution.py
@@ -338,9 +338,9 @@
         lax.fori_loop(0, rows // group, turn, 0)
 
     def body(t, carry):
+        stage(t, 3, relay_again)
+        stage(t, 1, relay)
         stage(t, 0, forward)
-        stage(t, 1, relay)
-        stage(t, 3, relay_again)
         stage(t, 5, compute)
         stage(t, 6, combine)
         stage(t, 7, combine_again)

time: 68.9 us -> 76 us (1.10)
  the two profiles are of different devices: /device:TPU:23 before, /device:TPU:15 now
where the time goes in v4:
time: 76 us; the launch traced here: 75.8 us
  Pallas kernels  69.5 us (91%)
  local copies, waits for them, and re-layouts  5.39 us (7%)
    pallas_call x1, Pallas kernels, local(): pl.pallas_call(functools.partial(kernel, nctx, nhead, chunks), out_shape=...  69.5 us
    unnamed x10, local copies, waits for them, and re-layouts  3.56 us
    another operation x2, local copies, waits for them, and re-layouts, local(): jnp.stack([a.transpose(1, 0, 2) for a in (keys, values, queries, out_grad)])  1.83 us

profile of v4, /device:TPU:15, one launch (start us, length us, event | category | flops | bytes accessed | tf_op | source)
XLA Modules:
  0.0 75.8 jit_solution(985718929527264492)
XLA Ops:
  0.6 0.0 copy-start.1
  0.6 0.0 copy-start.2
  0.7 1.6 %copy_bitcast_fusion = (bf16[1,16,128,128]{3,2,1,0:T(8,128)(2,1)S(1)}, bf16[1,16,128,128]{3,2,1,0:T(8,128)(2,1)S(1)}) fusion(bf16[128,16,128]{2,1,0:T(8,128)(2,1)} %param.8, bf16[128,16,128]{2,1,0:T(8,128)(2,1)} %param.5), kind=kLoop, calls=%fused_computation.1 | loop fusion | bytes 2097152 | tf_op jit(solution)/shard_map/stack | solution.py:380
  2.2 0.0 copy-done.1
  2.2 0.0 copy-done.2
  2.2 0.3 copy_bitcast_fusion.2
  2.5 0.0 copy-start
  2.5 0.3 pad_maximum_fusion.x_ref
  2.8 0.4 copy-done
  3.2 69.5 %shard_map.84 = (bf16[128,16,128]{2,1,0:T(8,128)(2,1)S(1)}, bf16[128,16,128]{2,1,0:T(8,128)(2,1)S(1)}, bf16[128,16,128]{2,1,0:T(8,128)(2,1)S(1)}, bf16[128,16,128]{2,1,0:T(8,128)(2,1)S(1)}) custom-call(s32[1,3]{1,0:T(1,128)S(1)} %copy-done, bf16[4,16,128,128]{3,2,1,0:T(8,128)(2,1)S(1)} %pad_maximum_fusion.x_ref), custom_call_target="tpu_custom_call" | custom-call | flops 3221225472 | bytes 4194304 | tf_op jit(solution)/shard_map/pallas_call | solution.py:384
  72.7 0.8 %copy.21 = bf16[128,16,128]{2,1,0:T(8,128)(2,1)} copy(bf16[128,16,128]{2,1,0:T(8,128)(2,1)S(1)} %get-tuple-element.12) | data formatting | bytes 1048576
  73.5 0.8 %copy.22 = bf16[128,16,128]{2,1,0:T(8,128)(2,1)} copy(bf16[128,16,128]{2,1,0:T(8,128)(2,1)S(1)} %get-tuple-element.13) | data formatting | bytes 1048576
  74.3 0.8 %copy.23 = bf16[128,16,128]{2,1,0:T(8,128)(2,1)} copy(bf16[128,16,128]{2,1,0:T(8,128)(2,1)S(1)} %get-tuple-element.14) | data formatting | bytes 1048576
  75.1 0.8 %copy.24 = bf16[128,16,128]{2,1,0:T(8,128)(2,1)} copy(bf16[128,16,128]{2,1,0:T(8,128)(2,1)S(1)} %get-tuple-element.15) | data formatting | bytes 1048576
Async XLA Ops:
  0.6 1.6 %copy-start.1 = (bf16[128,16,128]{2,1,0:T(8,128)(2,1)S(1)}, bf16[128,16,128]{2,1,0:T(8,128)(2,1)}, u32[]{:S(2)}) copy-start(bf16[128,16,128]{2,1,0:T(8,128)(2,1)} %param.7) | copy-start | bytes 1572868
  0.6 1.6 %copy-start.2 = (bf16[128,16,128]{2,1,0:T(8,128)(2,1)S(1)}, bf16[128,16,128]{2,1,0:T(8,128)(2,1)}, u32[]{:S(2)}) copy-start(bf16[128,16,128]{2,1,0:T(8,128)(2,1)} %param.6) | copy-start | bytes 1572868
  2.5 0.7 copy-start
